TPU v7x, 32 devices: a whole 2x2x4 slice. The times are simulated.
32 devices in a mesh: row: 16 (over z, x, core), col: 2 (over y).
Axes of the slice: x: 2, y: 2, z: 4, core: 2. Of those that a mesh axis runs over, the one named last changes fastest.
Arguments:
- covariance: float32 [16384, 16384], P('row', 'col'), may hold values from -6 to 6
- lon_courant: float32 [128, 128], replicated, may hold values from 0.05 to 0.95
- lat_courant: float32 [128, 128], replicated, may hold values from 0.05 to 0.9
- zonal_upwind_sign: int32 [128, 128], replicated, may hold values 0 or 1
- lat_sign: int32 [128, 128], replicated, may hold values 0 or 1
- cycle_counts: int32 [128], replicated, may hold values from 1 to 4
Outputs:
- forecast: float32 [16384, 16384], P('row', 'col')
Inputs may be any that keep to these rules, and one draw needn't show every extreme that they name: `zonal_upwind_sign`: 1 where the wind blows toward growing longitude, 0 otherwise. `lat_sign`: 1 where the wind blows toward growing latitude, 0 otherwise.
All inputs are finite; a program needn't handle non-finite values.
Results may differ from a plain program's by a relative error of at most 0.00002.
Values sent between devices are 32-bit elements; how exact they have to be, the bound alone decides.
No kernel may reach another device: no remote copies, remote signals or barrier semaphores. Data moves between devices by JAX's collectives and lax.ppermute only.
A program may use at most 320 MiB of HBM per device.

v0:
```python
import functools

import jax
import jax.numpy as jnp
from jax import lax
from jax.experimental import pallas as pl
from jax.experimental.pallas import tpu as pltpu
from jax.sharding import PartitionSpec as P

SUBCYCLES = 4
F32, BF16 = jnp.float32, jnp.bfloat16
LON_RATE, LAT_RATE, ZONAL, HEADING, COUNTS = range(5)
VMEM_BYTES = 56 * 1024 * 1024
HIGHEST = lax.Precision.HIGHEST


def split(values):
    high = values.astype(BF16)
    return high, (values - high.astype(F32)).astype(BF16)


def dot(left, right):
    return jnp.dot(left, right, preferred_element_type=F32)


def exact_dot(left, right):
    return jnp.dot(left, right, preferred_element_type=F32, precision=HIGHEST)


def blend(center, rate, sign, below, above):
    return center - rate * (center - jnp.where(sign > 0.5, below, above))


def table_row(tables, which, at):
    return tables[which, pl.ds(at, 1), :]


def zonal_bands(rate, sign, count):
    lons = rate.shape[-1]
    zero = jnp.zeros_like(rate)
    bands = {0: jnp.ones_like(rate)}
    for cycle in range(SUBCYCLES):
        cell = jnp.where(count > cycle, rate, 0.0)
        west = {k - 1: pltpu.roll(band, 1, 1) for k, band in bands.items()}
        east = {k + 1: pltpu.roll(band, lons - 1, 1) for k, band in bands.items()}
        bands = {
            k: blend(bands.get(k, zero), cell, sign, west.get(k, zero), east.get(k, zero))
            for k in range(-cycle - 1, cycle + 2)
        }
    return bands


def zonal_matrix(bands, lat):
    lons = bands[0].shape[-1]
    reach = lax.broadcasted_iota(jnp.int32, (lons, lons), 0) - lax.broadcasted_iota(jnp.int32, (lons, lons), 1)
    reach = jnp.where(reach < 0, reach + lons, reach)
    field = jnp.zeros((lons, lons), F32)
    for k, band in bands.items():
        field = jnp.where(reach == k % lons, band[lat:lat + 1, :], field)
    return field


def store_column_mats(bands, out, first, count):
    lons = bands[0].shape[-1]
    for lat in range(count):
        high, low = split(zonal_matrix(bands, lat))
        out[first + lat, :lons, :lons] = high
        out[first + lat, :lons, lons:] = low
        out[first + lat, lons:, :lons] = high
        out[first + lat, lons:, lons:] = jnp.zeros_like(low)


def column_tables_kernel(tables, out):
    bands = zonal_bands(tables[LON_RATE], tables[ZONAL], tables[COUNTS])
    store_column_mats(bands, out, 0, out.shape[0])


def padded(count, least):
    return -(-count // least) * least


def prepare_kernel(first_mat, blocks_last, *refs):
    sources, (row_part, col_part, first_part, mat_part, most, blocks, wide) = refs[:5], refs[5:]
    lats, lons = sources[0].shape
    wide[...] = jnp.zeros_like(wide)
    for which, source in enumerate(sources):
        values = source[...].astype(F32)
        if which == COUNTS:
            values = jnp.broadcast_to(values, (lons, lats)).T
        wide[which, 8:8 + lats, :] = values
    row_lats = row_part.shape[1] - 4
    col_lats = col_part.shape[1] - 4
    row = lax.axis_index("row")
    col_first = lax.axis_index("col") * col_lats
    odd = row % 2
    blocks[0] = odd * blocks_last
    blocks[1] = (1 - odd) * blocks_last
    blocks[2] = lax.axis_index("col") % 2
    for which in range(5):
        for out, first in ((row_part, row * row_lats + 6), (col_part, col_first + 6),
                           (first_part, col_first + first_mat + 7), (mat_part, col_first + 7)):
            out[which] = wide[which, pl.ds(first, out.shape[1]), :]
    heading = (sources[HEADING][...] == 1).astype(F32)
    upward = jnp.sum(heading, axis=1, keepdims=True)
    lat = lax.broadcasted_iota(jnp.int32, (lats, 1), 0)
    place = lat % (2 * row_lats)
    low = (place == 0) & (lat > 0)
    high = (place == 2 * row_lats - 1) & (lat < lats - 1)
    needed = jnp.where(low, upward, jnp.where(high, lons - upward, 0.0))
    most[0] = jnp.max(needed).astype(jnp.int32)


def early_tables_kernel(kept, blocks, tables, col_tables, covariance, col_mats, mats, rates, signs, pack_cross, add_cross,
                        chip_rows, *refs):
    lons = tables.shape[-1]
    side = 2 * lons
    cols = covariance.shape[1]
    *sent, passed, held, done = refs
    from_row = pl.multiple_of(blocks[1] * side, side)
    edges = [jnp.where(blocks[2] == at, cols - side, 0) for at in range(len(sent))]
    places = [(covariance.at[pl.ds(from_row, side), :], passed, chip_rows)]
    for at, edge in enumerate(edges):
        places.append((covariance.at[:, pl.ds(pl.multiple_of(edge, side), side)], held.at[at], sent[at]))
    loads = [pltpu.make_async_copy(source, spot, done.at[0, at]) for at, (source, spot, _) in enumerate(places)]
    stores = [pltpu.make_async_copy(spot, out, done.at[1, at]) for at, (_, spot, out) in enumerate(places)]
    for copy in loads:
        copy.start()

    def one(block, carry):
        first = pl.multiple_of(block * 8, 8)
        rows_here = [col_tables[which, pl.ds(first, 8), :] for which in (LON_RATE, ZONAL, COUNTS)]
        store_column_mats(zonal_bands(*rows_here), col_mats, first, 8)
        return carry

    lax.fori_loop(0, col_mats.shape[0] // 8, one, 0)
    for load, store in zip(loads, stores):
        load.wait()
        store.start()
    lats = mats.shape[0] - 2
    square = (lons, lons)
    down = lax.broadcasted_iota(jnp.int32, square, 0)
    across = lax.broadcasted_iota(jnp.int32, square, 1)

    def spread(which, at):
        return jnp.broadcast_to(table_row(tables, which, at), square).T

    low_mat = high_mat = None
    bands = zonal_bands(tables[LON_RATE], tables[ZONAL], tables[COUNTS])
    for lat in range(lats + 2):
        mat = zonal_matrix(bands, lat + 1).T
        if lat == 1:
            low_mat = mat
        if lat == lats:
            high_mat = mat
        high, low = split(mat)
        mats[lat, :lons, :lons] = high
        mats[lat, :lons, lons:] = high
        mats[lat, lons:, :lons] = low
        mats[lat, lons:, lons:] = jnp.zeros_like(low)
        rates[lat] = spread(LAT_RATE, lat + 1)
        signs[lat] = spread(HEADING, lat + 1)

    def packer(out, size, is_low):
        edge, beyond = (2, 1) if is_low else (lats + 1, lats + 2)
        mat = low_mat if is_low else high_mat
        wanted = not is_low
        rows = padded(2 * size, 16)
        sign = jnp.broadcast_to(table_row(tables, HEADING, beyond), square)
        mask = (sign > 0.5) == wanted
        rank = dot(mask.astype(BF16), (down <= across).astype(BF16))
        rank = jnp.where(mask, rank, 0.0)[:1]
        spot = lax.broadcasted_iota(jnp.int32, (rows, lons), 0)
        first = jnp.where(spot < size, spot, -2).astype(F32) + 1.0
        second = jnp.where((spot >= size) & (spot < 2 * size), spot - size, -2).astype(F32) + 1.0
        moved = exact_dot(jnp.where(rank == first, 1.0, 0.0), mat)
        raw = jnp.where(rank == second, 1.0, 0.0)
        rate = table_row(tables, LAT_RATE, edge)
        toward = (table_row(tables, HEADING, edge) > 0.5) == wanted
        own = moved * (1.0 - rate) + raw
        inner = moved * jnp.where(toward, rate, 0.0)
        high, low = split(jnp.concatenate([own, inner] if is_low else [inner, own], axis=1))
        span = 2 * lons
        extra = padded(size, 16)
        out[:rows, :span] = high
        out[:rows, span:] = high
        out[rows:, :span] = jnp.where(spot_below(size, extra, span), low[:extra].astype(F32), 0.0).astype(BF16)
        out[rows:, span:] = jnp.zeros((extra, span), BF16)

    def spot_below(size, extra, span):
        return lax.broadcasted_iota(jnp.int32, (extra, span), 0) < size

    def adder(out, size, is_low):
        edge, inner = (2, 3) if is_low else (lats + 1, lats)
        mat = low_mat if is_low else high_mat
        columns = padded(2 * size, 16)
        total = 3 * columns

        def wide(which, at):
            tile = spread(which, at)
            return jnp.concatenate([tile] * (-(-total // lons)), axis=1)[:, :total]

        mask = (wide(HEADING, edge) > 0.5) == is_low
        rank = jnp.where(mask, dot((across <= down).astype(BF16), mask.astype(BF16)), 0.0)
        place = lax.broadcasted_iota(jnp.int32, (lons, total), 1)
        spot = jnp.where(place >= columns, place - columns, place)
        spot = jnp.where(spot >= columns, spot - columns, spot)
        first = jnp.where(spot < size, spot, -2).astype(F32) + 1.0
        second = jnp.where((spot >= size) & (spot < 2 * size), spot - size, -2).astype(F32) + 1.0
        partial = jnp.where(rank == first, 1.0, 0.0)
        raw = jnp.where(rank == second, 1.0, 0.0)
        grown = exact_dot(mat * table_row(tables, LAT_RATE, edge), raw)
        rate = wide(LAT_RATE, edge)
        here = (1.0 - rate) * grown + rate * partial
        next_in = jnp.where((wide(HEADING, inner) > 0.5) == is_low, wide(LAT_RATE, inner), 0.0) * grown
        whole = jnp.concatenate([here, next_in] if is_low else [next_in, here], axis=0)
        high = whole.astype(BF16).astype(F32)
        place = lax.broadcasted_iota(jnp.int32, whole.shape, 1)
        middle = (place >= columns) & (place < 2 * columns)
        out[...] = jnp.where(middle, whole - high, high).astype(BF16)

    def sides(cross_low):
        packer(pack_cross, kept, cross_low)
        adder(add_cross, kept, cross_low)

    pl.when(blocks[0] == 0)(lambda: sides(True))
    pl.when(blocks[0] != 0)(lambda: sides(False))
    for copy in stores:
        copy.wait()


def sweep_columns(value, tables, first, mats, held, emit, group):
    lons = tables.shape[-1]

    def rate(k):
        return table_row(tables, LAT_RATE, first + 2 + k)

    def sign(k):
        return table_row(tables, HEADING, first + 2 + k)

    for k in range(-1, group + 1):
        start = blend(value(k), rate(k), sign(k), value(k - 1), value(k + 1))
        both = dot(jnp.concatenate(split(start), axis=1), mats(k + 1))
        held[:, (k + 1) * lons:(k + 2) * lons] = both[:, :lons] + both[:, lons:]
        if k >= 1:
            at = (k - 1) * lons
            below, center, above = (held[:, at + s * lons:at + (s + 1) * lons] for s in range(3))
            emit(k - 1, blend(center, rate(k - 1), sign(k - 1), below, above))


def edge_choice(step, last_step, halos, odd, rows):
    def outside(span, from_pair):
        pair = halos[0][rows, span]
        other = halos[1][rows, span] if len(halos) > 1 else jnp.zeros_like(pair)
        return jnp.where(from_pair, pair, other)

    def take(k, group, lons, low, main, high):
        if k < 0:
            span = slice((k + 2) * lons, (k + 3) * lons)
            inside = low[rows, span]
            return jnp.where(step == 0, outside(span, odd == 1), inside) if halos else inside
        if k < group:
            return main[rows, k * lons:(k + 1) * lons]
        span = slice((k - group) * lons, (k - group + 1) * lons)
        inside = high[rows, span]
        return jnp.where(step == last_step, outside(span, odd == 0), inside) if halos else inside

    return take


def pick_mats(main, first_extra, second_extra, group):
    def mats(at):
        if at < group:
            return main[at]
        return first_extra[0] if at == group else second_extra[0]

    return mats


def pack_kernel(group, place, steps_all, count, blocks, tables, mats, mats_a, mats_b, packer, low, main, high, *refs):
    halos = refs[:count]
    out, held, moved = refs[count:]
    lons = tables.shape[-1]
    step = place(pl.program_id(0))
    choose = edge_choice(step, steps_all - 1, halos, blocks[2], slice(None))

    def emit(k, values):
        moved[:, k * lons:(k + 1) * lons] = values

    sweep_columns(
        lambda k: choose(k, group, lons, low, main, high), tables, step * group,
        pick_mats(mats, mats_a, mats_b, group), held, emit, group,
    )
    sums = dot(packer[...], jnp.concatenate(split(moved[...]), axis=0))
    count = out.shape[0]
    rows = padded(count, 16)
    extra = padded(count // 2, 16)
    out[:extra] = sums[:extra] + sums[rows:]
    out[extra:] = sums[extra:count]


def local_kernel(group, steps_all, count, blocks, tables, mats, mats_a, mats_b, row_mats, rates, signs, low, main, high,
                 chip_low, chip_main, chip_high, chip_halos, *refs):
    halos = refs[:count]
    out, held, moved, stage = refs[-4:]
    lons = tables.shape[-1]
    side = 2 * lons
    step = pl.program_id(0)
    lats = row_mats.shape[0] - 2
    part = held.shape[0]
    weights = pick_mats(mats, mats_a, mats_b, group)
    chip_above = blocks[1] > 0
    top = (lats + 2) * lons

    @pl.when(pl.program_id(0) == 0)
    def _():
        moved[pl.ds(pl.multiple_of(jnp.where(chip_above, 0, top), lons), side), :] = jnp.zeros(
            (side, group * lons), F32
        )

    def sweep(value, held_here, first_row, count):
        def emit(k, values):
            moved[pl.ds(first_row, count), k * lons:(k + 1) * lons] = values

        sweep_columns(value, tables, step * group, weights, held_here, emit, group)

    def one(block, carry):
        first_row = pl.multiple_of(block * part, part)
        choose = edge_choice(step, steps_all - 1, halos, blocks[2], pl.ds(first_row, part))
        sweep(
            lambda k: choose(k, group, lons, low, main, high), held,
            pl.multiple_of(first_row + side, side), part,
        )
        return carry

    lax.fori_loop(0, main.shape[0] // part, one, 0)
    chip_sides = [chip_halos.at[:, at * side:(at + 1) * side] for at in range(count)]
    choose_chip = edge_choice(step, steps_all - 1, chip_sides, blocks[2], slice(None))
    sweep(
        lambda k: choose_chip(k, group, lons, chip_low, chip_main, chip_high), held.at[:side],
        pl.multiple_of(jnp.where(chip_above, top, 0), lons), side,
    )

    def wide(ref, at):
        return jnp.concatenate([ref[at]] * group, axis=1)

    def lat_of(ref, at):
        return ref[at * lons:(at + 1) * lons, :]

    for lat in range(-1, lats + 1):
        near = [lat_of(moved, at) for at in (lat + 1, lat + 2, lat + 3)]
        start = blend(near[1], wide(rates, lat + 1), wide(signs, lat + 1), near[0], near[2])
        both = dot(row_mats[lat + 1], jnp.concatenate(split(start), axis=0))
        stage[(lat + 1) * lons:(lat + 2) * lons, :] = both[:lons] + both[lons:]
        if lat >= 1:
            done = lat - 1
            below, center, above = (lat_of(stage, done + s) for s in range(3))
            out[done * lons:(done + 1) * lons, :] = blend(
                center, wide(rates, done + 1), wide(signs, done + 1), below, above
            )


def add_kernel(blocks, adder, received, before, after):
    columns = adder.shape[1] // 3
    values = received[...]
    if values.shape[0] < columns:
        rest = jnp.zeros((columns - values.shape[0], values.shape[1]), F32)
        values = jnp.concatenate([values, rest], axis=0)
    high, low = split(values)
    after[...] = before[...] + dot(adder[...], jnp.concatenate([high, high, low], axis=0))


def params():
    return pltpu.CompilerParams(vmem_limit_bytes=VMEM_BYTES)


def whole_spec(shape):
    return pl.BlockSpec(shape, lambda *_: (0,) * len(shape))


def mats_specs(group, place, side):
    return [
        pl.BlockSpec((group, side, side), lambda g, *_: (place(g), 0, 0)),
        pl.BlockSpec((1, side, side), lambda g, *_: (place(g) * group + group, 0, 0)),
        pl.BlockSpec((1, side, side), lambda g, *_: (place(g) * group + group + 1, 0, 0)),
    ]


def window_specs(rows, row_block, group, place, lons, col_blocks):
    half = group // 2
    return [
        pl.BlockSpec((rows, 2 * lons), lambda g, *_: (row_block(*_), jnp.maximum(place(g) * half - 1, 0))),
        pl.BlockSpec((rows, group * lons), lambda g, *_: (row_block(*_), place(g))),
        pl.BlockSpec((rows, 2 * lons), lambda g, *_: (row_block(*_), jnp.minimum((place(g) + 1) * half, col_blocks - 1))),
    ]


def largest_part(total, most):
    return max(part for part in range(1, most + 1) if total % part == 0)


def prepare(sources, counts, first_mat, blocks_last):
    lats, lons = sources[0].shape
    shapes = [jax.ShapeDtypeStruct((5, count, lons), F32) for count in counts]
    scalars = [jax.ShapeDtypeStruct((1,), jnp.int32), jax.ShapeDtypeStruct((3,), jnp.int32)]
    return pl.pallas_call(
        functools.partial(prepare_kernel, first_mat, blocks_last),
        in_specs=[whole_spec(t.shape) for t in sources],
        out_specs=[whole_spec(shape.shape) for shape in shapes] + [pl.BlockSpec(memory_space=pltpu.SMEM)] * 2,
        out_shape=shapes + scalars,
        scratch_shapes=[pltpu.VMEM((5, lats + 24, lons), F32)],
        compiler_params=params(),
        name="prepare",
    )(*sources)


def column_tables(tables, lons):
    total = tables.shape[1]
    return pl.pallas_call(
        column_tables_kernel,
        grid=(total // 8,),
        in_specs=[pl.BlockSpec((tables.shape[0], 8, lons), lambda g: (0, g, 0))],
        out_specs=pl.BlockSpec((8, 2 * lons, 2 * lons), lambda g: (g, 0, 0)),
        out_shape=jax.ShapeDtypeStruct((total, 2 * lons, 2 * lons), BF16),
        compiler_params=params(),
        name="column_tables",
    )(tables)


def early_tables(blocks, tables, col_tables, covariance, kept, count):
    rows, cols = covariance.shape
    lons = tables.shape[-1]
    lats = rows // lons
    side = 2 * lons
    shapes = [
        jax.ShapeDtypeStruct((col_tables.shape[1], side, side), BF16),
        jax.ShapeDtypeStruct((lats + 2, side, side), BF16),
        jax.ShapeDtypeStruct((lats + 2, lons, lons), F32),
        jax.ShapeDtypeStruct((lats + 2, lons, lons), F32),
        jax.ShapeDtypeStruct((padded(2 * kept, 16) + padded(kept, 16), 2 * side), BF16),
        jax.ShapeDtypeStruct((side, 3 * padded(2 * kept, 16)), BF16),
    ]
    copied = [jax.ShapeDtypeStruct((side, cols), F32)] + [jax.ShapeDtypeStruct((rows, side), F32)] * count
    here = pl.BlockSpec(memory_space=pl.ANY)
    return pl.pallas_call(
        functools.partial(early_tables_kernel, kept),
        in_specs=[
            pl.BlockSpec(memory_space=pltpu.SMEM), whole_spec(tables.shape), whole_spec(col_tables.shape), here,
        ],
        out_specs=[whole_spec(shape.shape) for shape in shapes] + [here] * len(copied),
        out_shape=shapes + copied,
        scratch_shapes=[
            pltpu.VMEM((side, cols), F32),
            pltpu.VMEM((count, rows, side), F32),
            pltpu.SemaphoreType.DMA((2, count + 1)),
        ],
        compiler_params=params(),
        name="early_tables",
    )(blocks, tables, col_tables, covariance)


def pack_call(blocks, covariance, tables, mats, mats_first, packer, halos, group, chunk, kept):
    rows, cols = covariance.shape
    lons = tables.shape[-1]
    side = 2 * lons
    steps_all = cols // (group * lons)
    first, steps = chunk

    def place(g):
        return lax.rem(first + g, steps_all)

    def mats_place(g):
        return place(g) - mats_first

    specs = [whole_spec(tables.shape)] + mats_specs(group, mats_place, side) + [whole_spec(packer.shape)]
    specs += window_specs(side, lambda b: b[0], group, place, lons, cols // side)
    specs += [pl.BlockSpec((side, side), lambda g, b: (b[0], 0))] * len(halos)
    return pl.pallas_call(
        functools.partial(pack_kernel, group, place, steps_all, len(halos)),
        grid_spec=pltpu.PrefetchScalarGridSpec(
            num_scalar_prefetch=1,
            grid=(steps,),
            in_specs=specs,
            out_specs=pl.BlockSpec((2 * kept, group * lons), lambda g, *_: (0, g)),
            scratch_shapes=[pltpu.VMEM((side, (group + 2) * lons), F32), pltpu.VMEM((side, group * lons), F32)],
        ),
        out_shape=jax.ShapeDtypeStruct((2 * kept, steps * group * lons), F32),
        compiler_params=params(),
        name="pack_edges",
    )(blocks, tables, mats, mats, mats, packer, covariance, covariance, covariance, *halos)


def local_call(blocks, covariance, tables, mats, row_mats, rates, signs, halos, chip_rows, chip_halos, group):
    rows, cols = covariance.shape
    lons = tables.shape[-1]
    side = 2 * lons
    part = largest_part(rows // side, 2) * side

    steps = cols // (group * lons)

    def place(g):
        return g

    specs = [whole_spec(tables.shape)] + mats_specs(group, place, side)
    specs += [whole_spec(row_mats.shape), whole_spec(rates.shape), whole_spec(signs.shape)]
    specs += window_specs(rows, lambda *_: 0, group, place, lons, cols // side)
    specs += window_specs(side, lambda *_: 0, group, place, lons, cols // side)
    specs += [whole_spec(chip_halos.shape)] + [whole_spec((rows, side))] * len(halos)
    args = [blocks, tables, mats, mats, mats, row_mats, rates, signs, covariance, covariance, covariance]
    args += [chip_rows, chip_rows, chip_rows, chip_halos, *halos]
    return pl.pallas_call(
        functools.partial(local_kernel, group, steps, len(halos)),
        grid_spec=pltpu.PrefetchScalarGridSpec(
            num_scalar_prefetch=1,
            grid=(steps,),
            in_specs=specs,
            out_specs=pl.BlockSpec((rows, group * lons), lambda g, *_: (0, place(g))),
            scratch_shapes=[
                pltpu.VMEM((part, (group + 2) * lons), F32),
                pltpu.VMEM((rows + 2 * side, group * lons), F32),
                pltpu.VMEM((rows + side, group * lons), F32),
            ],
        ),
        out_shape=jax.ShapeDtypeStruct((rows, cols), F32),
        compiler_params=params(),
        name="local_forecast",
    )(*args)


def add_call(blocks, forecast, adder, received, chunk, group):
    side = adder.shape[0]
    width = group * side // 2
    first, steps = chunk
    steps_all = forecast.shape[1] // width
    spot = pl.BlockSpec((side, width), lambda g, b: (b[0], lax.rem(first + g, steps_all)))
    return pl.pallas_call(
        add_kernel,
        grid_spec=pltpu.PrefetchScalarGridSpec(
            num_scalar_prefetch=1,
            grid=(steps,),
            in_specs=[
                whole_spec(adder.shape),
                pl.BlockSpec((received.shape[0], width), lambda g, b: (0, g)),
                spot,
            ],
            out_specs=spot,
        ),
        out_shape=jax.ShapeDtypeStruct(forecast.shape, F32),
        input_output_aliases={3: 0},
        compiler_params=params(),
        name="add_edges",
    )(blocks, adder, received, forecast)


def chunks_of(steps_all):
    if steps_all < 4:
        return [(0, steps_all)]
    start = max(1, (steps_all - 2) // 3)
    middle = steps_all - 2 - start
    return [(1, start), (1 + start, middle), (1 + start + middle, steps_all - start - middle)]


def swaps(axis, start):
    count = lax.axis_size(axis)
    pairs = [(i, i + 1) for i in range(start, count - 1, 2)]
    return pairs + [(b, a) for a, b in pairs]


def forecast_with(kept, covariance, blocks, row_part, col_part, first_part, mat_part):
    rows, cols = covariance.shape
    lons = row_part.shape[-1]
    side = 2 * lons
    group = largest_part(cols // lons, 8)
    steps_all = cols // (group * lons)
    chunks = chunks_of(steps_all)
    cross, chip = swaps("row", 1), swaps("row", 0)
    col_swaps = [pairs for pairs in (swaps("col", 0), swaps("col", 1)) if pairs]
    first_mats, row_mats, rates, signs, packer, adder, chip_rows, *sides = early_tables(
        blocks, row_part, first_part, covariance, kept, len(col_swaps)
    )
    halos = [lax.ppermute(sent, "col", pairs) for sent, pairs in zip(sides, col_swaps)]
    arrived = []

    def pack(chunk, mats, mats_first, halos=()):
        return pack_call(blocks, covariance, col_part, mats, mats_first, packer, halos, group, chunk, kept)

    def send(packed):
        arrived.append(lax.ppermute(packed, "row", cross))

    early = len(chunks) > 1
    if early:
        packed = pack(chunks[0], first_mats, chunks[0][0])
        packed, chip_rows, mat_part = lax.optimization_barrier((packed, chip_rows, mat_part))
        send(packed)
    chip_rows = lax.ppermute(chip_rows, "row", chip)
    mats = column_tables(mat_part, lons)
    for chunk in chunks[early:-1]:
        packed, arrived[0], halos = lax.optimization_barrier((pack(chunk, mats, 0), arrived[0], halos))
        send(packed)
    near = [lax.dynamic_slice_in_dim(halo, blocks[1] * side, side, 0) for halo in halos]
    chip_halos = lax.ppermute(jnp.concatenate(near, axis=1), "row", chip)
    packed, row_mats = lax.optimization_barrier((pack(chunks[-1], mats, 0, halos), row_mats))
    send(packed)
    forecast = local_call(
        blocks, covariance, col_part, mats, row_mats, rates, signs, halos, chip_rows, chip_halos, group
    )
    for chunk, received in zip(chunks, arrived):
        forecast = add_call(blocks, forecast, adder, received, chunk, group)
    return forecast


def per_device(covariance, lon_courant, lat_courant, zonal_upwind_sign, lat_sign, cycle_counts):
    rows, cols = covariance.shape
    lons = lon_courant.shape[1]
    row_lats, col_lats = rows // lons, cols // lons
    group = largest_part(col_lats, 8)
    chunk = chunks_of(col_lats // group)[0]
    counts = (row_lats + 4, col_lats + 4, padded(chunk[1] * group + 2, 8), padded(col_lats + 2, 8))
    sources = (lon_courant, lat_courant, zonal_upwind_sign, lat_sign, cycle_counts[None, :])
    *parts, most, blocks = prepare(sources, counts, chunk[0] * group, rows // (2 * lons) - 1)
    sizes = [lons * part // 32 for part in (19, 22, 32)]
    branch = sum((most[0] > size).astype(jnp.int32) for size in sizes[:-1])
    return lax.switch(
        branch, [functools.partial(forecast_with, size) for size in sizes],
        covariance, blocks, *parts,
    )


def solution(mesh):
    placed = (P("row", "col"), P(), P(), P(), P(), P())
    return jax.shard_map(
        per_device, mesh=mesh, in_specs=placed, out_specs=P("row", "col"), check_vma=False
    )
```

profile of v0, /device:TPU:1, one launch (start us, length us, event | category | flops | bytes accessed | tf_op | source)
XLA Modules:
  0.0 139.1 jit_solution(4838202846570348605)
XLA Ops:
  0.0 1.6 %prepare.1 = (f32[5,12,128]{2,1,0:T(8,128)S(1)}, f32[5,68,128]{2,1,0:T(8,128)S(1)}, f32[5,24,128]{2,1,0:T(8,128)S(1)}, f32[5,72,128]{2,1,0:T(8,128)S(1)}, s32[1]{0:T(128)}, /*index=5*/s32[3]{0:T(128)S(1)}) custom-call(f32[128,128]{1,0:T(8,128)} %refs_0_.1, f32[128,128]{1,0:T(8,128)} %refs_1_.1, s32[128,128]{1,0:T(8,128)} %refs_2_.1, s32[128,128]{1,0:T(8,128)} %refs_3_.1, ...), custom_call_target="tpu_custom_call" | custom-call | tf_op jit(solution)/shard_map/prepare/pallas_call | solution.py:405
  2.9 136.2 %conditional.1 = (f32[1024,8192]{1,0:T(8,128)}) conditional(s32[]{:T(128)} %bitcast.4, (s32[3]{0:T(128)S(1)}, f32[5,12,128]{2,1,0:T(8,128)S(1)}, f32[5,24,128]{2,1,0:T(8,128)S(1)}, f32[1024,8192]{1,0:T(8,128)}, f32[5,68,128]{2,1,0:T(8,128)S(1)}, /*index=5*/f32[5,72,128]{2,1,0:T(8,128)S(1)}) %tuple.23, (s32[3]{0:T(128)S(1)}, ...), branch_computations={%region_0.0_spmd, %region_1.0_spmd, %region_2.0_spmd} | conditional | flops 4 | bytes 99090880 | solution.py:622
  2.9 10.4 %early_tables.3 = (bf16[24,256,256]{2,1,0:T(8,128)(2,1)}, bf16[10,256,256]{2,1,0:T(8,128)(2,1)}, f32[10,128,128]{2,1,0:T(8,128)}, f32[10,128,128]{2,1,0:T(8,128)...) custom-call(s32[3]{0:T(128)S(1)} %get-tuple-element.44.blocks, ...), custom_call_target="tpu_custom_call" | custom-call | tf_op jit(solution)/shard_map/cond/branch_0_fun/early_tables/pallas_call | solution.py:444
  13.4 0.0 copy-start.12
  13.4 5.4 %pack_edges.9 = f32[152,2048]{1,0:T(8,128)} custom-call(s32[3]{0:T(128)S(1)} %get-tuple-element.44.blocks, f32[5,68,128]{2,1,0:T(8,128)S(1)} %get-tuple-element.50.tables, bf16[24,256,256]{2,1,0:T(8,128)(2,1)} %get-tuple-element.51.mats.mats_a.mats_b, bf16[24,256,256]{2,1,0:T(8,128)(2,1)} %get-tuple-element.51.mats.mats_a.mats_b, ...), custom_call_target="tpu_custom_call" | custom-call | tf_op jit(solution)/shard_map/cond/branch_0_fun/pack_edges/pallas_call | solution.py:477
  18.7 0.1 collective-permute-start.4
  18.8 4.5 %collective-permute-start = (f32[152,2048]{1,0:T(8,128)}, f32[152,2048]{1,0:T(8,128)S(1)}, u32[]{:S(2)}, u32[]{:S(2)}) collective-permute-start(f32[152,2048]{1,0:T(8,128)} %pack_edges.9), channel_id=1, source_target_pairs={{2,4},{6,8},{10,12},{14,16},{18,20},{22,24},{26,28},{4,2},{8,6},{1... | collective-permute-start | bytes 3735560 | tf_op jit(solution)/shard_map/cond/branch_0_fun/ppermute | solution.py:587
  23.3 0.0 copy-done.12
  23.3 1.3 collective-permute-start.1
  24.6 8.5 %column_tables.3.mats.mats_a.mats_b = bf16[72,256,256]{2,1,0:T(8,128)(2,1)} custom-call(f32[5,72,128]{2,1,0:T(8,128)S(1)} %get-tuple-element.55.tables), custom_call_target="tpu_custom_call" | custom-call | tf_op jit(solution)/shard_map/cond/branch_0_fun/column_tables/pallas_call | solution.py:418
  33.0 8.6 %pack_edges.10 = f32[152,4096]{1,0:T(8,128)} custom-call(s32[3]{0:T(128)S(1)} %get-tuple-element.44.blocks, f32[5,68,128]{2,1,0:T(8,128)S(1)} %get-tuple-element.50.tables, bf16[72,256,256]{2,1,0:T(8,128)(2,1)} %column_tables.3.mats.mats_a.mats_b, bf16[72,256,256]{2,1,0:T(8,128)(2,1)} %column_tables.3.mats.mats_a.mats_b, ...), custom_call_target="tpu_custom_call" | custom-call | tf_op jit(solution)/shard_map/cond/branch_0_fun/pack_edges/pallas_call | solution.py:477
  41.6 4.3 %collective-permute-done.1.refs_0_ = f32[1024,256]{1,0:T(8,128)S(1)} collective-permute-done((f32[1024,256]{1,0:T(8,128)S(1)}, f32[1024,256]{1,0:T(8,128)S(1)}, u32[]{:S(2)}, u32[]{:S(2)}) %collective-permute-start.1) | collective-permute-done | bytes 1048608 | tf_op jit(solution)/shard_map/cond/branch_0_fun/ppermute | solution.py:580
  45.9 0.0 copy-start
  45.9 4.8 %collective-permute-done.received = f32[152,2048]{1,0:T(8,128)S(1)} collective-permute-done((f32[152,2048]{1,0:T(8,128)}, f32[152,2048]{1,0:T(8,128)S(1)}, u32[]{:S(2)}, u32[]{:S(2)}) %collective-permute-start) | collective-permute-done | bytes 1245216 | tf_op jit(solution)/shard_map/cond/branch_0_fun/ppermute | solution.py:587
  50.7 0.0 copy-start.7
  50.7 4.3 %collective-permute-start.3 = (f32[152,4096]{1,0:T(8,128)}, f32[152,4096]{1,0:T(8,128)}, u32[]{:S(2)}, u32[]{:S(2)}) collective-permute-start(f32[152,4096]{1,0:T(8,128)} %pack_edges.10), channel_id=1, source_target_pairs={{2,4},{6,8},{10,12},{14,16},{18,20},{22,24},{26,28},{4,2},{8,6},{1... | collective-permute-start | bytes 7471112 | tf_op jit(solution)/shard_map/cond/branch_0_fun/ppermute | solution.py:587
  55.0 0.0 copy-done
  55.0 5.5 %pack_edges.11 = f32[152,2048]{1,0:T(8,128)} custom-call(s32[3]{0:T(128)S(1)} %get-tuple-element.44.blocks, f32[5,68,128]{2,1,0:T(8,128)S(1)} %get-tuple-element.50.tables, bf16[72,256,256]{2,1,0:T(8,128)(2,1)} %column_tables.3.mats.mats_a.mats_b, bf16[72,256,256]{2,1,0:T(8,128)(2,1)} %column_tables.3.mats.mats_a.mats_b, ...), custom_call_target="tpu_custom_call" | custom-call | tf_op jit(solution)/shard_map/cond/branch_0_fun/pack_edges/pallas_call | solution.py:477
  60.6 0.0 copy-done.7
  60.6 2.1 %collective-permute-start.2 = (f32[152,2048]{1,0:T(8,128)}, f32[152,2048]{1,0:T(8,128)S(1)}, u32[]{:S(2)}, u32[]{:S(2)}) collective-permute-start(f32[152,2048]{1,0:T(8,128)} %pack_edges.11), channel_id=1, source_target_pairs={{2,4},{6,8},{10,12},{14,16},{18,20},{22,24},{26,28},{4,2},{8,6},{1... | collective-permute-start | bytes 3735560 | tf_op jit(solution)/shard_map/cond/branch_0_fun/ppermute | solution.py:587
  62.7 0.6 slice.6
  63.9 1.0 constant_dynamic-slice_fusion
  64.9 0.1 collective-permute-start.5
  65.0 1.5 %collective-permute-done.5.chip_halos = f32[256,256]{1,0:T(8,128)S(1)} collective-permute-done((f32[256,256]{1,0:T(8,128)S(1)}, f32[256,256]{1,0:T(8,128)S(1)}, u32[]{:S(2)}, u32[]{:S(2)}) %collective-permute-start.5) | collective-permute-done | bytes 262176 | tf_op jit(solution)/shard_map/cond/branch_0_fun/ppermute | solution.py:600
  66.5 0.0 copy-start.9
  66.5 0.0 collective-permute-done.4.chip_low.chip_main.chip_high
  66.5 0.7 copy-done.9
  67.2 56.2 %local_forecast.3.before = f32[1024,8192]{1,0:T(8,128)} custom-call(s32[3]{0:T(128)S(1)} %get-tuple-element.44.blocks, f32[5,68,128]{2,1,0:T(8,128)S(1)} %get-tuple-element.50.tables, bf16[72,256,256]{2,1,0:T(8,128)(2,1)} %column_tables.3.mats.mats_a.mats_b, bf16[72,256,256]{2,1,0:T(8,128)(2,1)} %column_tables.3.mats.mats_a.mats_b, ...), custom_call_target="tpu_custom_call" | custom-call | tf_op jit(solution)/shard_map/cond/branch_0_fun/local_forecast/pallas_call | solution.py:510
  123.4 4.0 %add_edges.9.before = f32[1024,8192]{1,0:T(8,128)} custom-call(s32[3]{0:T(128)S(1)} %get-tuple-element.44.blocks, bf16[256,480]{1,0:T(8,128)(2,1)} %get-tuple-element.49.adder, f32[152,2048]{1,0:T(8,128)} %copy-done.7, f32[1024,8192]{1,0:T(8,128)} %local_forecast.3.before), custom_call_target="tpu_custom_call", output_to_operand_aliasing={{}: (3, {})} | custom-call | tf_op jit(solution)/shard_map/cond/branch_0_fun/add_edges/pallas_call | solution.py:535
  127.4 0.0 collective-permute-done.3.received
  127.4 6.6 %add_edges.10.before = f32[1024,8192]{1,0:T(8,128)} custom-call(s32[3]{0:T(128)S(1)} %get-tuple-element.44.blocks, bf16[256,480]{1,0:T(8,128)(2,1)} %get-tuple-element.49.adder, f32[152,4096]{1,0:T(8,128)} %collective-permute-done.3.received, f32[1024,8192]{1,0:T(8,128)} %add_edges.9.before), custom_call_target="tpu_custom_call", output_to_operand_aliasing={{}: (3, {})} | custom-call | tf_op jit(solution)/shard_map/cond/branch_0_fun/add_edges/pallas_call | solution.py:535
  134.0 0.0 collective-permute-done.2.received
  134.0 0.0 copy-start.8
  134.0 1.1 copy-done.8
  135.1 4.0 %add_edges.11 = f32[1024,8192]{1,0:T(8,128)} custom-call(s32[3]{0:T(128)S(1)} %get-tuple-element.44.blocks, bf16[256,480]{1,0:T(8,128)(2,1)} %get-tuple-element.49.adder, f32[152,2048]{1,0:T(8,128)} %copy-done.8, f32[1024,8192]{1,0:T(8,128)} %add_edges.10.before), custom_call_target="tpu_custom_call", output_to_operand_aliasing={{}: (3, {})} | custom-call | tf_op jit(solution)/shard_map/cond/branch_0_fun/add_edges/pallas_call | solution.py:535
Async XLA Ops:
  13.4 9.9 %copy-start.12 = (f32[1024,256]{1,0:T(8,128)S(1)}, f32[1024,256]{1,0:T(8,128)}, u32[]{:S(2)}) copy-start(f32[1024,256]{1,0:T(8,128)} %get-tuple-element.57) | copy-start | bytes 3145732 | tf_op jit(solution)/shard_map/cond
  18.7 47.7 %collective-permute-start.4 = (f32[256,8192]{1,0:T(8,128)}, f32[256,8192]{1,0:T(8,128)}, u32[]{:S(2)}, u32[]{:S(2)}) collective-permute-start(f32[256,8192]{1,0:T(8,128)} %get-tuple-element.66), channel_id=1, source_target_pairs={{0,2},{4,6},{8,10},{12,14},{16,18},{20,22},{24,26},{28,30},{2,0},{... | collective-permute-start | bytes 25165832 | tf_op jit(solution)/shard_map/cond/branch_0_fun/ppermute | solution.py:594
  18.8 31.9 %collective-permute-start = (f32[152,2048]{1,0:T(8,128)}, f32[152,2048]{1,0:T(8,128)S(1)}, u32[]{:S(2)}, u32[]{:S(2)}) collective-permute-start(f32[152,2048]{1,0:T(8,128)} %pack_edges.9), channel_id=1, source_target_pairs={{2,4},{6,8},{10,12},{14,16},{18,20},{22,24},{26,28},{4,2},{8,6},{1... | collective-permute-start | bytes 3735560 | tf_op jit(solution)/shard_map/cond/branch_0_fun/ppermute | solution.py:587
  23.3 22.6 %collective-permute-start.1 = (f32[1024,256]{1,0:T(8,128)S(1)}, f32[1024,256]{1,0:T(8,128)S(1)}, u32[]{:S(2)}, u32[]{:S(2)}) collective-permute-start(f32[1024,256]{1,0:T(8,128)S(1)} %copy-done.12), channel_id=1, source_target_pairs={{0,1},{1,0},{2,3},{3,2},{4,5},{5,4},{6,7},{7,6},{8,9},{9,8},{10,11... | collective-permute-start | bytes 3145736 | tf_op jit(solution)/shard_map/cond/branch_0_fun/ppermute | solution.py:580
  45.9 9.1 %copy-start = (f32[1024,256]{1,0:T(8,128)}, f32[1024,256]{1,0:T(8,128)S(1)}, u32[]{:S(2)}) copy-start(f32[1024,256]{1,0:T(8,128)S(1)} %collective-permute-done.1.refs_0_) | copy-start | bytes 3145732 | tf_op jit(solution)/shard_map/cond
  50.7 9.8 %copy-start.7 = (f32[152,2048]{1,0:T(8,128)}, f32[152,2048]{1,0:T(8,128)S(1)}, u32[]{:S(2)}) copy-start(f32[152,2048]{1,0:T(8,128)S(1)} %collective-permute-done.received) | copy-start | bytes 3735556 | tf_op jit(solution)/shard_map/cond
  50.7 76.7 %collective-permute-start.3 = (f32[152,4096]{1,0:T(8,128)}, f32[152,4096]{1,0:T(8,128)}, u32[]{:S(2)}, u32[]{:S(2)}) collective-permute-start(f32[152,4096]{1,0:T(8,128)} %pack_edges.10), channel_id=1, source_target_pairs={{2,4},{6,8},{10,12},{14,16},{18,20},{22,24},{26,28},{4,2},{8,6},{1... | collective-permute-start | bytes 7471112 | tf_op jit(solution)/shard_map/cond/branch_0_fun/ppermute | solution.py:587
  60.6 73.5 %collective-permute-start.2 = (f32[152,2048]{1,0:T(8,128)}, f32[152,2048]{1,0:T(8,128)S(1)}, u32[]{:S(2)}, u32[]{:S(2)}) collective-permute-start(f32[152,2048]{1,0:T(8,128)} %pack_edges.11), channel_id=1, source_target_pairs={{2,4},{6,8},{10,12},{14,16},{18,20},{22,24},{26,28},{4,2},{8,6},{1... | collective-permute-start | bytes 3735560 | tf_op jit(solution)/shard_map/cond/branch_0_fun/ppermute | solution.py:587
  64.9 1.6 %collective-permute-start.5 = (f32[256,256]{1,0:T(8,128)S(1)}, f32[256,256]{1,0:T(8,128)S(1)}, u32[]{:S(2)}, u32[]{:S(2)}) collective-permute-start(f32[256,256]{1,0:T(8,128)S(1)} %constant_dynamic-slice_fusion), channel_id=1, source_target_pairs={{0,2},{4,6},{8,10},{12,14},{16,18},{20,22},{24,26},{28,30},{2,0},{... | collective-permute-start | bytes 786440 | tf_op jit(solution)/shard_map/cond/branch_0_fun/ppermute | solution.py:600
  66.5 0.7 copy-start.9
  134.0 1.1 copy-start.8
where the time goes:
time: 139 us
  Pallas kernels  111 us (80%)
  starting transfers between devices  12.3 us (9%)
  waiting for transfers between devices  10.7 us (8%)
  local copies, waits for them, and re-layouts  3.36 us (2%)
    pallas_call x1, Pallas kernels, local_call(): pl.pallas_call(functools.partial(local_kernel, group, steps, len(halos)),...  56.2 us
    pallas_call x3, Pallas kernels, pack_call(): pl.pallas_call(functools.partial(pack_kernel, group, place, steps_all, le...  19.4 us
    pallas_call x3, Pallas kernels, add_call(): pl.pallas_call(add_kernel, grid_spec=pltpu.PrefetchScalarGridSpec(num_sca...  14.6 us
    ppermute x3, starting transfers between devices, send(): arrived.append(lax.ppermute(packed, 'row', cross))  10.8 us
    pallas_call x1, Pallas kernels, early_tables(): pl.pallas_call(functools.partial(early_tables_kernel, kept), in_specs=[pl...  10.4 us
    pallas_call x1, Pallas kernels, column_tables(): pl.pallas_call(column_tables_kernel, grid=(total // 8,), in_specs=[pl.Blo...  8.45 us
    ppermute x3, waiting for transfers between devices, send(): arrived.append(lax.ppermute(packed, 'row', cross))  4.83 us
    ppermute x1, waiting for transfers between devices, forecast_with(): lax.ppermute(sent, 'col', pairs)  4.33 us
  transfers between devices with their start and end apart: 6, of which 3 were waited for; matrix products, arithmetic and copies ran while one was open for 1% of the time, Pallas kernels for 64%

commit v1 on v0

--- a/solution.py
+++ b/solution.py
@@ -528,8 +528,8 @@
 
 def add_call(blocks, forecast, adder, received, chunk, group):
     side = adder.shape[0]
-    width = group * side // 2
-    first, steps = chunk
+    width = group * side // 4
+    first, steps = (2 * count for count in chunk)
     steps_all = forecast.shape[1] // width
     spot = pl.BlockSpec((side, width), lambda g, b: (b[0], lax.rem(first + g, steps_all)))
     return pl.pallas_call(

time: 139 us -> 144 us (1.036)
  Pallas kernels: 111 us -> 115 us
    pallas_call x3, Pallas kernels: 14.6 us -> 19 us  [add_call(): pl.pallas_call(add_kernel, grid_spec=pltpu.PrefetchScalarGridSpec(num_sca...]
  transfers between devices with their start and end apart: 6 -> 6, of which waited for: 3 -> 3; matrix products, arithmetic and copies ran while one was open for 1% -> 1% of each run, Pallas kernels for 64% -> 65%
where the time goes in v1:
time: 144 us
  Pallas kernels  115 us (80%)
  starting transfers between devices  12.3 us (9%)
  waiting for transfers between devices  10.7 us (7%)
  local copies, waits for them, and re-layouts  3.36 us (2%)
    pallas_call x1, Pallas kernels, local_call(): pl.pallas_call(functools.partial(local_kernel, group, steps, len(halos)),...  56.2 us
    pallas_call x3, Pallas kernels, pack_call(): pl.pallas_call(functools.partial(pack_kernel, group, place, steps_all, le...  19.4 us
    pallas_call x3, Pallas kernels, add_call(): pl.pallas_call(add_kernel, grid_spec=pltpu.PrefetchScalarGridSpec(num_sca...  19 us
    ppermute x3, starting transfers between devices, send(): arrived.append(lax.ppermute(packed, 'row', cross))  10.8 us
    pallas_call x1, Pallas kernels, early_tables(): pl.pallas_call(functools.partial(early_tables_kernel, kept), in_specs=[pl...  10.4 us
    pallas_call x1, Pallas kernels, column_tables(): pl.pallas_call(column_tables_kernel, grid=(total // 8,), in_specs=[pl.Blo...  8.45 us
    ppermute x3, waiting for transfers between devices, send(): arrived.append(lax.ppermute(packed, 'row', cross))  4.83 us
    ppermute x1, waiting for transfers between devices, forecast_with(): lax.ppermute(sent, 'col', pairs)  4.33 us
  transfers between devices with their start and end apart: 6, of which 3 were waited for; matrix products, arithmetic and copies ran while one was open for 1% of the time, Pallas kernels for 65%

profile of v1, /device:TPU:1, one launch (start us, length us, event | category | flops | bytes accessed | tf_op | source)
XLA Modules:
  0.0 143.5 jit_solution(1836910918383089576)
XLA Ops:
  0.0 1.6 %prepare.1 = (f32[5,12,128]{2,1,0:T(8,128)S(1)}, f32[5,68,128]{2,1,0:T(8,128)S(1)}, f32[5,24,128]{2,1,0:T(8,128)S(1)}, f32[5,72,128]{2,1,0:T(8,128)S(1)}, s32[1]{0:T(128)}, /*index=5*/s32[3]{0:T(128)S(1)}) custom-call(f32[128,128]{1,0:T(8,128)} %refs_0_.1, f32[128,128]{1,0:T(8,128)} %refs_1_.1, s32[128,128]{1,0:T(8,128)} %refs_2_.1, s32[128,128]{1,0:T(8,128)} %refs_3_.1, ...), custom_call_target="tpu_custom_call" | custom-call | tf_op jit(solution)/shard_map/prepare/pallas_call | solution.py:405
  2.9 140.6 %conditional.1 = (f32[1024,8192]{1,0:T(8,128)}) conditional(s32[]{:T(128)} %bitcast.4, (s32[3]{0:T(128)S(1)}, f32[5,12,128]{2,1,0:T(8,128)S(1)}, f32[5,24,128]{2,1,0:T(8,128)S(1)}, f32[1024,8192]{1,0:T(8,128)}, f32[5,68,128]{2,1,0:T(8,128)S(1)}, /*index=5*/f32[5,72,128]{2,1,0:T(8,128)S(1)}) %tuple.23, (s32[3]{0:T(128)S(1)}, ...), branch_computations={%region_0.0_spmd, %region_1.0_spmd, %region_2.0_spmd} | conditional | flops 4 | bytes 99090880 | solution.py:622
  2.9 10.4 %early_tables.3 = (bf16[24,256,256]{2,1,0:T(8,128)(2,1)}, bf16[10,256,256]{2,1,0:T(8,128)(2,1)}, f32[10,128,128]{2,1,0:T(8,128)}, f32[10,128,128]{2,1,0:T(8,128)...) custom-call(s32[3]{0:T(128)S(1)} %get-tuple-element.44.blocks, ...), custom_call_target="tpu_custom_call" | custom-call | tf_op jit(solution)/shard_map/cond/branch_0_fun/early_tables/pallas_call | solution.py:444
  13.4 0.0 copy-start.12
  13.4 5.4 %pack_edges.9 = f32[152,2048]{1,0:T(8,128)} custom-call(s32[3]{0:T(128)S(1)} %get-tuple-element.44.blocks, f32[5,68,128]{2,1,0:T(8,128)S(1)} %get-tuple-element.50.tables, bf16[24,256,256]{2,1,0:T(8,128)(2,1)} %get-tuple-element.51.mats.mats_a.mats_b, bf16[24,256,256]{2,1,0:T(8,128)(2,1)} %get-tuple-element.51.mats.mats_a.mats_b, ...), custom_call_target="tpu_custom_call" | custom-call | tf_op jit(solution)/shard_map/cond/branch_0_fun/pack_edges/pallas_call | solution.py:477
  18.7 0.1 collective-permute-start.4
  18.8 4.5 %collective-permute-start = (f32[152,2048]{1,0:T(8,128)}, f32[152,2048]{1,0:T(8,128)S(1)}, u32[]{:S(2)}, u32[]{:S(2)}) collective-permute-start(f32[152,2048]{1,0:T(8,128)} %pack_edges.9), channel_id=1, source_target_pairs={{2,4},{6,8},{10,12},{14,16},{18,20},{22,24},{26,28},{4,2},{8,6},{1... | collective-permute-start | bytes 3735560 | tf_op jit(solution)/shard_map/cond/branch_0_fun/ppermute | solution.py:587
  23.3 0.0 copy-done.12
  23.3 1.3 collective-permute-start.1
  24.6 8.5 %column_tables.3.mats.mats_a.mats_b = bf16[72,256,256]{2,1,0:T(8,128)(2,1)} custom-call(f32[5,72,128]{2,1,0:T(8,128)S(1)} %get-tuple-element.55.tables), custom_call_target="tpu_custom_call" | custom-call | tf_op jit(solution)/shard_map/cond/branch_0_fun/column_tables/pallas_call | solution.py:418
  33.0 8.6 %pack_edges.10 = f32[152,4096]{1,0:T(8,128)} custom-call(s32[3]{0:T(128)S(1)} %get-tuple-element.44.blocks, f32[5,68,128]{2,1,0:T(8,128)S(1)} %get-tuple-element.50.tables, bf16[72,256,256]{2,1,0:T(8,128)(2,1)} %column_tables.3.mats.mats_a.mats_b, bf16[72,256,256]{2,1,0:T(8,128)(2,1)} %column_tables.3.mats.mats_a.mats_b, ...), custom_call_target="tpu_custom_call" | custom-call | tf_op jit(solution)/shard_map/cond/branch_0_fun/pack_edges/pallas_call | solution.py:477
  41.6 4.3 %collective-permute-done.1.refs_0_ = f32[1024,256]{1,0:T(8,128)S(1)} collective-permute-done((f32[1024,256]{1,0:T(8,128)S(1)}, f32[1024,256]{1,0:T(8,128)S(1)}, u32[]{:S(2)}, u32[]{:S(2)}) %collective-permute-start.1) | collective-permute-done | bytes 1048608 | tf_op jit(solution)/shard_map/cond/branch_0_fun/ppermute | solution.py:580
  45.9 0.0 copy-start
  45.9 4.8 %collective-permute-done.received = f32[152,2048]{1,0:T(8,128)S(1)} collective-permute-done((f32[152,2048]{1,0:T(8,128)}, f32[152,2048]{1,0:T(8,128)S(1)}, u32[]{:S(2)}, u32[]{:S(2)}) %collective-permute-start) | collective-permute-done | bytes 1245216 | tf_op jit(solution)/shard_map/cond/branch_0_fun/ppermute | solution.py:587
  50.7 0.0 copy-start.7
  50.7 4.3 %collective-permute-start.3 = (f32[152,4096]{1,0:T(8,128)}, f32[152,4096]{1,0:T(8,128)}, u32[]{:S(2)}, u32[]{:S(2)}) collective-permute-start(f32[152,4096]{1,0:T(8,128)} %pack_edges.10), channel_id=1, source_target_pairs={{2,4},{6,8},{10,12},{14,16},{18,20},{22,24},{26,28},{4,2},{8,6},{1... | collective-permute-start | bytes 7471112 | tf_op jit(solution)/shard_map/cond/branch_0_fun/ppermute | solution.py:587
  55.0 0.0 copy-done
  55.0 5.5 %pack_edges.11 = f32[152,2048]{1,0:T(8,128)} custom-call(s32[3]{0:T(128)S(1)} %get-tuple-element.44.blocks, f32[5,68,128]{2,1,0:T(8,128)S(1)} %get-tuple-element.50.tables, bf16[72,256,256]{2,1,0:T(8,128)(2,1)} %column_tables.3.mats.mats_a.mats_b, bf16[72,256,256]{2,1,0:T(8,128)(2,1)} %column_tables.3.mats.mats_a.mats_b, ...), custom_call_target="tpu_custom_call" | custom-call | tf_op jit(solution)/shard_map/cond/branch_0_fun/pack_edges/pallas_call | solution.py:477
  60.6 0.0 copy-done.7
  60.6 2.1 %collective-permute-start.2 = (f32[152,2048]{1,0:T(8,128)}, f32[152,2048]{1,0:T(8,128)S(1)}, u32[]{:S(2)}, u32[]{:S(2)}) collective-permute-start(f32[152,2048]{1,0:T(8,128)} %pack_edges.11), channel_id=1, source_target_pairs={{2,4},{6,8},{10,12},{14,16},{18,20},{22,24},{26,28},{4,2},{8,6},{1... | collective-permute-start | bytes 3735560 | tf_op jit(solution)/shard_map/cond/branch_0_fun/ppermute | solution.py:587
  62.7 0.6 slice.6
  63.9 1.0 constant_dynamic-slice_fusion
  64.9 0.1 collective-permute-start.5
  65.0 1.5 %collective-permute-done.5.chip_halos = f32[256,256]{1,0:T(8,128)S(1)} collective-permute-done((f32[256,256]{1,0:T(8,128)S(1)}, f32[256,256]{1,0:T(8,128)S(1)}, u32[]{:S(2)}, u32[]{:S(2)}) %collective-permute-start.5) | collective-permute-done | bytes 262176 | tf_op jit(solution)/shard_map/cond/branch_0_fun/ppermute | solution.py:600
  66.5 0.0 copy-start.9
  66.5 0.0 collective-permute-done.4.chip_low.chip_main.chip_high
  66.5 0.7 copy-done.9
  67.2 56.2 %local_forecast.3.before = f32[1024,8192]{1,0:T(8,128)} custom-call(s32[3]{0:T(128)S(1)} %get-tuple-element.44.blocks, f32[5,68,128]{2,1,0:T(8,128)S(1)} %get-tuple-element.50.tables, bf16[72,256,256]{2,1,0:T(8,128)(2,1)} %column_tables.3.mats.mats_a.mats_b, bf16[72,256,256]{2,1,0:T(8,128)(2,1)} %column_tables.3.mats.mats_a.mats_b, ...), custom_call_target="tpu_custom_call" | custom-call | tf_op jit(solution)/shard_map/cond/branch_0_fun/local_forecast/pallas_call | solution.py:510
  123.4 5.2 %add_edges.9.before = f32[1024,8192]{1,0:T(8,128)} custom-call(s32[3]{0:T(128)S(1)} %get-tuple-element.44.blocks, bf16[256,480]{1,0:T(8,128)(2,1)} %get-tuple-element.49.adder, f32[152,2048]{1,0:T(8,128)} %copy-done.7, f32[1024,8192]{1,0:T(8,128)} %local_forecast.3.before), custom_call_target="tpu_custom_call", output_to_operand_aliasing={{}: (3, {})} | custom-call | tf_op jit(solution)/shard_map/cond/branch_0_fun/add_edges/pallas_call | solution.py:535
  128.6 0.0 collective-permute-done.3.received
  128.6 8.7 %add_edges.10.before = f32[1024,8192]{1,0:T(8,128)} custom-call(s32[3]{0:T(128)S(1)} %get-tuple-element.44.blocks, bf16[256,480]{1,0:T(8,128)(2,1)} %get-tuple-element.49.adder, f32[152,4096]{1,0:T(8,128)} %collective-permute-done.3.received, f32[1024,8192]{1,0:T(8,128)} %add_edges.9.before), custom_call_target="tpu_custom_call", output_to_operand_aliasing={{}: (3, {})} | custom-call | tf_op jit(solution)/shard_map/cond/branch_0_fun/add_edges/pallas_call | solution.py:535
  137.3 0.0 collective-permute-done.2.received
  137.3 0.0 copy-start.8
  137.3 1.1 copy-done.8
  138.4 5.2 %add_edges.11 = f32[1024,8192]{1,0:T(8,128)} custom-call(s32[3]{0:T(128)S(1)} %get-tuple-element.44.blocks, bf16[256,480]{1,0:T(8,128)(2,1)} %get-tuple-element.49.adder, f32[152,2048]{1,0:T(8,128)} %copy-done.8, f32[1024,8192]{1,0:T(8,128)} %add_edges.10.before), custom_call_target="tpu_custom_call", output_to_operand_aliasing={{}: (3, {})} | custom-call | tf_op jit(solution)/shard_map/cond/branch_0_fun/add_edges/pallas_call | solution.py:535
Async XLA Ops:
  13.4 9.9 %copy-start.12 = (f32[1024,256]{1,0:T(8,128)S(1)}, f32[1024,256]{1,0:T(8,128)}, u32[]{:S(2)}) copy-start(f32[1024,256]{1,0:T(8,128)} %get-tuple-element.57) | copy-start | bytes 3145732 | tf_op jit(solution)/shard_map/cond
  18.7 47.7 %collective-permute-start.4 = (f32[256,8192]{1,0:T(8,128)}, f32[256,8192]{1,0:T(8,128)}, u32[]{:S(2)}, u32[]{:S(2)}) collective-permute-start(f32[256,8192]{1,0:T(8,128)} %get-tuple-element.66), channel_id=1, source_target_pairs={{0,2},{4,6},{8,10},{12,14},{16,18},{20,22},{24,26},{28,30},{2,0},{... | collective-permute-start | bytes 25165832 | tf_op jit(solution)/shard_map/cond/branch_0_fun/ppermute | solution.py:594
  18.8 31.9 %collective-permute-start = (f32[152,2048]{1,0:T(8,128)}, f32[152,2048]{1,0:T(8,128)S(1)}, u32[]{:S(2)}, u32[]{:S(2)}) collective-permute-start(f32[152,2048]{1,0:T(8,128)} %pack_edges.9), channel_id=1, source_target_pairs={{2,4},{6,8},{10,12},{14,16},{18,20},{22,24},{26,28},{4,2},{8,6},{1... | collective-permute-start | bytes 3735560 | tf_op jit(solution)/shard_map/cond/branch_0_fun/ppermute | solution.py:587
  23.3 22.6 %collective-permute-start.1 = (f32[1024,256]{1,0:T(8,128)S(1)}, f32[1024,256]{1,0:T(8,128)S(1)}, u32[]{:S(2)}, u32[]{:S(2)}) collective-permute-start(f32[1024,256]{1,0:T(8,128)S(1)} %copy-done.12), channel_id=1, source_target_pairs={{0,1},{1,0},{2,3},{3,2},{4,5},{5,4},{6,7},{7,6},{8,9},{9,8},{10,11... | collective-permute-start | bytes 3145736 | tf_op jit(solution)/shard_map/cond/branch_0_fun/ppermute | solution.py:580
  45.9 9.1 %copy-start = (f32[1024,256]{1,0:T(8,128)}, f32[1024,256]{1,0:T(8,128)S(1)}, u32[]{:S(2)}) copy-start(f32[1024,256]{1,0:T(8,128)S(1)} %collective-permute-done.1.refs_0_) | copy-start | bytes 3145732 | tf_op jit(solution)/shard_map/cond
  50.7 9.8 %copy-start.7 = (f32[152,2048]{1,0:T(8,128)}, f32[152,2048]{1,0:T(8,128)S(1)}, u32[]{:S(2)}) copy-start(f32[152,2048]{1,0:T(8,128)S(1)} %collective-permute-done.received) | copy-start | bytes 3735556 | tf_op jit(solution)/shard_map/cond
  50.7 77.8 %collective-permute-start.3 = (f32[152,4096]{1,0:T(8,128)}, f32[152,4096]{1,0:T(8,128)}, u32[]{:S(2)}, u32[]{:S(2)}) collective-permute-start(f32[152,4096]{1,0:T(8,128)} %pack_edges.10), channel_id=1, source_target_pairs={{2,4},{6,8},{10,12},{14,16},{18,20},{22,24},{26,28},{4,2},{8,6},{1... | collective-permute-start | bytes 7471112 | tf_op jit(solution)/shard_map/cond/branch_0_fun/ppermute | solution.py:587
  60.6 76.7 %collective-permute-start.2 = (f32[152,2048]{1,0:T(8,128)}, f32[152,2048]{1,0:T(8,128)S(1)}, u32[]{:S(2)}, u32[]{:S(2)}) collective-permute-start(f32[152,2048]{1,0:T(8,128)} %pack_edges.11), channel_id=1, source_target_pairs={{2,4},{6,8},{10,12},{14,16},{18,20},{22,24},{26,28},{4,2},{8,6},{1... | collective-permute-start | bytes 3735560 | tf_op jit(solution)/shard_map/cond/branch_0_fun/ppermute | solution.py:587
  64.9 1.6 %collective-permute-start.5 = (f32[256,256]{1,0:T(8,128)S(1)}, f32[256,256]{1,0:T(8,128)S(1)}, u32[]{:S(2)}, u32[]{:S(2)}) collective-permute-start(f32[256,256]{1,0:T(8,128)S(1)} %constant_dynamic-slice_fusion), channel_id=1, source_target_pairs={{0,2},{4,6},{8,10},{12,14},{16,18},{20,22},{24,26},{28,30},{2,0},{... | collective-permute-start | bytes 786440 | tf_op jit(solution)/shard_map/cond/branch_0_fun/ppermute | solution.py:600
  66.5 0.7 copy-start.9
  137.3 1.1 copy-start.8
